TPU v7x, 128 devices: a whole 4x4x4 slice. The times are simulated.
128 devices in a mesh: section: 2 (over z_hi), render: 4 (over z_lo, core), dp: 16 (over y, x).
Axes of the slice: x: 4, y: 4, z: 4 (z_hi: 2, z_lo: 2; z = z_hi * 2 + z_lo), core: 2. Of those that a mesh axis runs over, the one named last changes fastest.
Arguments:
- section_tokens: bfloat16 [2, 16, 512, 2048], P('section', 'dp', 'render'), may hold values from -60 to 60
- w_qkv: bfloat16 [2, 2048, 3072], P('section', 'dp'), may hold values from -0.5 to 0.5
- w_out: bfloat16 [2, 1024, 2048], P('section', 'dp'), may hold values from -0.1875 to 0.1875
- gains: float32 [2, 2048], P('section'), may hold values from 0.25 to 1.75
- cotangent: bfloat16 [16, 512, 2048], P('dp', 'render'), may hold values from -6 to 6
Outputs:
- token_grads: bfloat16 [2, 16, 512, 2048], P('section', 'dp', 'render')
- qkv_grads: float32 [2, 2048, 3072], P('section', 'dp')
- out_grads: float32 [2, 1024, 2048], P('section', 'dp')
- gain_grads: float32 [2, 2048], P('section')
All inputs are finite; a program needn't handle non-finite values.
Results may differ from a plain program's by a relative error of at most 0.02.
Values may be sent and summed in bfloat16 or wider, within the bound.
No kernel may reach another device: no remote copies, remote signals or barrier semaphores. Data moves between devices by JAX's collectives and lax.ppermute only.
A program may use at most 192 MiB of HBM per device.

v0:
```python
import jax
import jax.numpy as jnp
from jax import lax
from jax.sharding import PartitionSpec as P

HEADS = 8
HD = 128
NORM_EPSILON = 1e-06


def joined_along(blocks, dim):
    blocks = jnp.moveaxis(blocks, 0, dim)
    lengths = blocks.shape
    return blocks.reshape(*lengths[:dim], lengths[dim] * lengths[dim + 1], *lengths[dim + 2 :])


def sent_to_all(shard, axis):
    peers = lax.axis_size(axis)
    return lax.all_to_all(
        jnp.broadcast_to(shard[None], (peers, *shard.shape)), axis, 0, 0, tiled=True
    )


def gather_directly(shard, axis, dim):
    return joined_along(sent_to_all(shard, axis), dim)


def shifted(block, axis, distance):
    devices = range(lax.axis_size(axis))
    route = [(i - distance, i) for i in devices if i - distance in devices]
    return lax.ppermute(block, axis, route)


def split_up(shard, dim, peers):
    lengths = shard.shape
    blocks = shard.reshape(*lengths[:dim], peers, lengths[dim] // peers, *lengths[dim + 1 :])
    return jnp.moveaxis(blocks, dim, 0)


def sum_at_owner(shard, axis, dim):
    blocks = split_up(shard, dim, lax.axis_size(axis))
    arrived = lax.all_to_all(blocks, axis, split_axis=0, concat_axis=0, tiled=True)
    return arrived.astype(jnp.float32).sum(axis=0)


def sent_together(arrays, axis, dim, along):
    widths = [a.shape[along] for a in arrays]
    both = jnp.concatenate(arrays, axis=along)
    out = lax.all_gather(both, axis, axis=dim, tiled=True)
    return tuple(jnp.split(out, [sum(widths[:k]) for k in range(1, len(widths))], axis=along))


def sum_packed(arrays, axis, dims):
    peers = lax.axis_size(axis)
    blocks = [split_up(a, dim, peers) for a, dim in zip(arrays, dims)]
    lines = jnp.concatenate([b.reshape(peers, -1) for b in blocks], axis=1)
    span = max(16, -(-lines.shape[1] // 1024) * 8)
    lines = jnp.pad(lines, ((0, 0), (0, span * 128 - lines.shape[1]))).reshape(-1, 128)
    line, at, finished = (lax.psum_scatter(lines, axis, tiled=True).reshape(-1), 0, [])
    for b in blocks:
        part = b[0]
        finished.append(line[at : at + part.size].reshape(part.shape))
        at += part.size
    return tuple(finished)


def gather_packed(arrays, axis, dims):
    line = jnp.concatenate([a.reshape(-1) for a in arrays])
    lines, at, finished = (lax.all_gather(line, axis), 0, [])
    for a, dim in zip(arrays, dims):
        blocks = lines[:, at : at + a.size].reshape(-1, *a.shape)
        finished.append(joined_along(blocks, dim))
        at += a.size
    return tuple(finished)


def over_copies(shard, axis):
    return sent_to_all(shard, axis).sum(axis=0)


def rms_norm(values, gain_row):
    wide_rows = values.astype(jnp.float32)
    row_scale = lax.rsqrt(jnp.mean(wide_rows * wide_rows, axis=-1, keepdims=True) + NORM_EPSILON)
    return ((wide_rows * row_scale * gain_row).astype(jnp.bfloat16), row_scale)


def norm_back(values, row_scale, gain_row, upstream):
    wide_rows = values.astype(jnp.float32)
    grad_wide = upstream.astype(jnp.float32)
    scaled = grad_wide * gain_row
    inner_sum = jnp.sum(scaled * wide_rows, axis=-1, keepdims=True)
    result = row_scale * scaled - wide_rows * row_scale**3 * inner_sum / values.shape[-1]
    gain_term = jnp.sum(grad_wide * wide_rows * row_scale, axis=0)
    return (result, gain_term)


def split_heads(values):
    return values.reshape(values.shape[0], HEADS, HD)


def only_when(flag, compute):

    def skipped():
        return jax.tree.map(jnp.zeros_like, compute())

    return lax.cond(flag, compute, skipped)


def attend(queries, key_rows, value_rows):
    factor = HD ** (-0.5)
    scores = (
        jnp.einsum(
            "qhd,khd->hqk",
            split_heads(queries),
            split_heads(key_rows),
            preferred_element_type=jnp.float32,
        )
        * factor
    )
    row_top = jnp.max(scores, axis=-1, keepdims=True)
    raised = jnp.exp(scores - row_top)
    row_total = jnp.sum(raised, axis=-1, keepdims=True)
    attn_prob = raised / row_total
    mixed_heads = jnp.einsum(
        "hqk,khd->qhd",
        attn_prob.astype(jnp.bfloat16),
        split_heads(value_rows),
        preferred_element_type=jnp.float32,
    )
    return (
        mixed_heads.reshape(queries.shape[0], HEADS * HD).astype(jnp.bfloat16),
        attn_prob,
        row_top,
        row_total,
    )


def score_grad(attn_prob, upstream, value_rows):
    factor = HD ** (-0.5)
    grad_prob = jnp.einsum(
        "qhd,khd->hqk",
        split_heads(upstream),
        split_heads(value_rows),
        preferred_element_type=jnp.float32,
    )
    row_delta = jnp.sum(grad_prob * attn_prob, axis=-1, keepdims=True)
    grad_score = (attn_prob * (grad_prob - row_delta) * factor).astype(jnp.bfloat16)
    return (grad_score, row_delta)


def key_terms_of(grad_score, attn_prob, queries, upstream):
    grad_key = jnp.einsum(
        "hqk,qhd->khd", grad_score, split_heads(queries), preferred_element_type=jnp.float32
    )
    grad_value = jnp.einsum(
        "hqk,qhd->khd",
        attn_prob.astype(jnp.bfloat16),
        split_heads(upstream),
        preferred_element_type=jnp.float32,
    )
    key_count = grad_key.shape[0]
    return (grad_key.reshape(key_count, HEADS * HD), grad_value.reshape(key_count, HEADS * HD))


def key_side(queries, upstream, row_top, row_total, row_delta, key_rows, value_rows):
    factor = HD ** (-0.5)
    scores = (
        jnp.einsum(
            "qhd,khd->hqk",
            split_heads(queries),
            split_heads(key_rows),
            preferred_element_type=jnp.float32,
        )
        * factor
    )
    attn_prob = jnp.exp(scores - row_top) / row_total
    grad_prob = jnp.einsum(
        "qhd,khd->hqk",
        split_heads(upstream),
        split_heads(value_rows),
        preferred_element_type=jnp.float32,
    )
    grad_score = (attn_prob * (grad_prob - row_delta) * factor).astype(jnp.bfloat16)
    grad_key, grad_value = key_terms_of(grad_score, attn_prob, queries, upstream)
    return jnp.concatenate([grad_key, grad_value], 1).astype(jnp.bfloat16)


def shards(section_tokens, w_qkv, w_out, gains, cotangent):
    tokens = section_tokens[0, 0]
    upstream = cotangent[0]
    gain_row = gains[0]
    head_width = HEADS * HD
    half_rows = tokens.shape[0] // 2
    section_index = lax.axis_index("section")
    is_encoder = section_index == 0
    is_decoder = jnp.logical_not(is_encoder)
    full_qkv, full_out = (
        lax.all_gather(w_qkv[0], "dp", axis=0, tiled=True),
        lax.all_gather(w_out[0], "dp", axis=0, tiled=True),
    )
    normed, row_scale = rms_norm(tokens, gain_row)
    projected = jnp.dot(normed, full_qkv, preferred_element_type=jnp.float32).astype(jnp.bfloat16)
    own_kv = projected[:, head_width:]
    enc_query = projected[half_rows:, :head_width]
    all_kv = gather_directly(own_kv, "render", 0)

    def encoder_forward():
        enc_mixed, enc_prob, enc_top, enc_total = attend(
            enc_query, all_kv[:, :head_width], all_kv[:, head_width:]
        )
        latent = (
            tokens[half_rows:].astype(jnp.float32)
            + jnp.dot(enc_mixed, full_out, preferred_element_type=jnp.float32)
        ).astype(jnp.bfloat16)
        return (enc_mixed, enc_prob, enc_top, enc_total, latent)

    enc_mixed, enc_prob, enc_top, enc_total, latent = only_when(is_encoder, encoder_forward)
    arrived = shifted(latent, "section", 1)

    def latent_project():
        lat_norm, lat_scale = rms_norm(arrived, gain_row)
        lat_kv = jnp.dot(
            lat_norm, full_qkv[:, head_width:], preferred_element_type=jnp.float32
        ).astype(jnp.bfloat16)
        return (lat_norm, lat_scale, lat_kv)

    lat_norm, lat_scale, lat_kv = only_when(is_decoder, latent_project)
    scene_kv = gather_directly(lat_kv, "render", 0)
    lat_count = scene_kv.shape[0]

    def decoder_attention():
        key_rows = jnp.concatenate(
            [scene_kv[:, :head_width], projected[:, head_width : 2 * head_width]], 0
        )
        value_rows = jnp.concatenate([scene_kv[:, head_width:], projected[:, 2 * head_width :]], 0)
        dec_query = projected[:, :head_width]
        dec_mixed, dec_prob, dec_top, dec_total = attend(dec_query, key_rows, value_rows)
        dec_out_part = jnp.einsum(
            "nc,nd->cd", dec_mixed, upstream, preferred_element_type=jnp.float32
        ).astype(jnp.bfloat16)
        grad_mixed = jnp.einsum(
            "nd,cd->nc", upstream, full_out, preferred_element_type=jnp.float32
        ).astype(jnp.bfloat16)
        dec_score, dec_delta = score_grad(dec_prob, grad_mixed, value_rows)
        dec_grad_query = jnp.einsum(
            "hqk,khd->qhd", dec_score, split_heads(key_rows), preferred_element_type=jnp.float32
        ).reshape(dec_query.shape[0], head_width)
        dec_grad_key, dec_grad_value = key_terms_of(dec_score, dec_prob, dec_query, grad_mixed)
        lat_terms = jnp.concatenate([dec_grad_key[:lat_count], dec_grad_value[:lat_count]], 1)
        dec_grad_proj = jnp.concatenate(
            [dec_grad_query, dec_grad_key[lat_count:], dec_grad_value[lat_count:]], 1
        ).astype(jnp.bfloat16)
        return (lat_terms, dec_grad_proj, dec_out_part)

    lat_terms, dec_grad_proj, dec_out_part = only_when(is_decoder, decoder_attention)
    lat_grad = sum_at_owner(lat_terms.astype(jnp.bfloat16), "render", 0).astype(jnp.bfloat16)

    def decoder_finish():
        dec_qkv_part = jnp.einsum(
            "nd,nc->dc", normed, dec_grad_proj, preferred_element_type=jnp.float32
        )
        lat_weight_part = jnp.einsum(
            "nd,nc->dc", lat_norm, lat_grad, preferred_element_type=jnp.float32
        )
        dec_qkv_part = dec_qkv_part.at[:, head_width:].add(lat_weight_part).astype(jnp.bfloat16)
        grad_normed = jnp.einsum(
            "nc,dc->nd", dec_grad_proj, full_qkv, preferred_element_type=jnp.float32
        ).astype(jnp.bfloat16)
        grad_lat_norm = jnp.einsum(
            "nc,dc->nd", lat_grad, full_qkv[:, head_width:], preferred_element_type=jnp.float32
        ).astype(jnp.bfloat16)
        dec_back, dec_gain_first = norm_back(tokens, row_scale, gain_row, grad_normed)
        dec_result = (upstream.astype(jnp.float32) + dec_back).astype(jnp.bfloat16)
        lat_back, dec_gain_second = norm_back(arrived, lat_scale, gain_row, grad_lat_norm)
        return (
            dec_qkv_part,
            dec_result,
            lat_back.astype(jnp.bfloat16),
            dec_gain_first + dec_gain_second,
        )

    dec_qkv_part, dec_result, lat_back, dec_gain = only_when(is_decoder, decoder_finish)
    returned = shifted(lat_back, "section", -1)

    def encoder_back_queries():
        enc_values = all_kv[:, head_width:]
        enc_keys = all_kv[:, :head_width]
        enc_out_part = jnp.einsum(
            "nc,nd->cd", enc_mixed, returned, preferred_element_type=jnp.float32
        ).astype(jnp.bfloat16)
        grad_enc_mixed = jnp.einsum(
            "nd,cd->nc", returned, full_out, preferred_element_type=jnp.float32
        ).astype(jnp.bfloat16)
        enc_score, enc_delta = score_grad(enc_prob, grad_enc_mixed, enc_values)
        query_grad = (
            jnp.einsum(
                "hqk,khd->qhd", enc_score, split_heads(enc_keys), preferred_element_type=jnp.float32
            )
            .reshape(half_rows, head_width)
            .astype(jnp.bfloat16)
        )
        return (enc_out_part, grad_enc_mixed, enc_delta, query_grad)

    enc_out_part, grad_enc_mixed, enc_delta, query_grad = only_when(
        is_encoder, encoder_back_queries
    )
    all_query, all_upstream = sent_together((enc_query, grad_enc_mixed), "render", 0, 1)
    all_top, all_total, all_delta = sent_together((enc_top, enc_total, enc_delta), "render", 1, 0)

    def own_key_grads():
        return key_side(
            all_query,
            all_upstream,
            all_top,
            all_total,
            all_delta,
            own_kv[:, :head_width],
            own_kv[:, head_width:],
        )

    key_grad = only_when(is_encoder, own_key_grads)

    def encoder_finish():
        query_weight_part = jnp.einsum(
            "nd,nc->dc", normed[half_rows:], query_grad, preferred_element_type=jnp.float32
        )
        key_weight_part = jnp.einsum(
            "nd,nc->dc", normed, key_grad, preferred_element_type=jnp.float32
        )
        enc_qkv_part = jnp.concatenate([query_weight_part, key_weight_part], 1).astype(jnp.bfloat16)
        grad_enc_norm = jnp.einsum(
            "nc,dc->nd", key_grad, full_qkv[:, head_width:], preferred_element_type=jnp.float32
        )
        query_back = jnp.einsum(
            "nc,dc->nd", query_grad, full_qkv[:, :head_width], preferred_element_type=jnp.float32
        )
        grad_enc_norm = grad_enc_norm.at[half_rows:].add(query_back).astype(jnp.bfloat16)
        enc_back, enc_gain_term = norm_back(tokens, row_scale, gain_row, grad_enc_norm)
        enc_result = enc_back.at[half_rows:].add(returned.astype(jnp.float32)).astype(jnp.bfloat16)
        return (enc_qkv_part, enc_result, enc_gain_term)

    enc_qkv_part, enc_result, enc_gain_term = only_when(is_encoder, encoder_finish)
    token_grad = jnp.where(is_encoder, enc_result, dec_result)
    qkv_part = jnp.where(is_encoder, enc_qkv_part, dec_qkv_part).astype(jnp.float32)
    out_part = jnp.where(is_encoder, enc_out_part, dec_out_part).astype(jnp.float32)
    gain_part = jnp.where(is_encoder, enc_gain_term, dec_gain)
    qkv_total, out_total = (
        lax.psum_scatter(
            qkv_part.astype(jnp.bfloat16), "render", scatter_dimension=1, tiled=True
        ).astype(jnp.float32),
        lax.psum_scatter(
            out_part.astype(jnp.bfloat16), "render", scatter_dimension=1, tiled=True
        ).astype(jnp.float32),
    )
    qkv_total, out_total = tuple(
        (
            part.astype(jnp.float32)
            for part in sum_packed(
                (qkv_total.astype(jnp.bfloat16), out_total.astype(jnp.bfloat16)), "dp", (0, 0)
            )
        )
    )
    qkv_total, out_total = tuple(
        (
            part.astype(jnp.float32)
            for part in gather_packed(
                (qkv_total.astype(jnp.bfloat16), out_total.astype(jnp.bfloat16)), "render", (1, 1)
            )
        )
    )
    gain_total = over_copies(gain_part, ("render", "dp"))
    return (token_grad[None, None], qkv_total[None], out_total[None], gain_total[None])


def solution(mesh):
    in_specs = (
        P("section", "dp", "render", None),
        P("section", "dp", None),
        P("section", "dp", None),
        P("section", None),
        P("dp", "render", None),
    )
    out_specs = (
        P("section", "dp", "render", None),
        P("section", "dp", None),
        P("section", "dp", None),
        P("section", None),
    )
    return jax.shard_map(shards, mesh=mesh, in_specs=in_specs, out_specs=out_specs, check_vma=False)
```

profile of v0, /device:TPU:1, one launch (start us, length us, event | category | flops | bytes accessed | tf_op | source)
XLA Modules:
  0.0 694.2 jit_solution(12119105009085443958)
XLA Ops:
  11.1 92.1 %all-gather.10.cloned.1.call-done = bf16[1,2048,3072]{2,1,0:T(8,128)(2,1)} async-done(((bf16[1,128,3072]{2,1,0:T(8,128)(2,1)}), bf16[1,2048,3072]{2,1,0:T(8,128)(2,1)}) %all-gather.10.cloned.1.call-update) | async-done | bytes 12582928 | tf_op jit(solution)/shard_map/all_gather | solution.py:198
  103.3 6.4 convolution_convert_fusion.11
  111.6 5.1 all-to-all-start
  117.4 24.3 %all-to-all-done = bf16[4,128,2048]{1,2,0:T(8,128)(2,1)} async-done(((bf16[4,128,2048]{1,2,0:T(8,128)(2,1)}), bf16[4,128,2048]{1,2,0:T(8,128)(2,1)}, u32[]{:S(2)}, u32[]{:S(2)}) %all-to-all-start) | async-done | bytes 2097184 | tf_op jit(solution)/shard_map/all_to_all | solution.py:19
  144.6 12.0 %all-gather.12.cloned.1.call-done = bf16[1,1024,2048]{2,1,0:T(8,128)(2,1)} async-done(((bf16[1,64,2048]{2,1,0:T(8,128)(2,1)}), bf16[1,1024,2048]{2,1,0:T(8,128)(2,1)}) %all-gather.12.cloned.1.call-update) | async-done | bytes 4194320 | tf_op jit(solution)/shard_map/all_gather | solution.py:199
  156.5 13.9 %conditional.7 = (bf16[64,1024]{1,0:T(8,128)(2,1)}, f32[8,64,512]{2,1,0:T(8,128)}, f32[8,64,1]{1,0,2:T(8,128)}, f32[8,64,1]{1,0,2:T(8,128)}, bf16[64,2048]{1,0:T(8,128)(2,1)S(1)}) conditional(s32[]{:T(128)} %convert_element_type.206, () %tuple.79, (bf16[64,1024]{1,0:T(8,128)(2,1)}, bf16[512,2048]{1,0:T(8,128)(2,1)S(1)}, ...), branch_computations={%region_1.0_spmd, %region_2.0_spmd} | conditional | flops 404945920 | bytes 37890116 | solution.py:106
  172.5 5.6 collective-permute-done
  179.9 5.4 all-to-all-start.1
  185.4 13.7 %all-to-all-done.1 = bf16[4,64,2048]{2,1,0:T(8,128)(2,1)} async-done(((bf16[4,64,2048]{2,1,0:T(8,128)(2,1)}), bf16[4,64,2048]{2,1,0:T(8,128)(2,1)}, u32[]{:S(2)}, u32[]{:S(2)}) %all-to-all-start.1) | async-done | bytes 1048608 | tf_op jit(solution)/shard_map/all_to_all | solution.py:19
  199.1 5.0 conditional.9
  206.4 5.1 all-to-all-start.2
  211.5 13.7 %all-to-all-done.2 = bf16[4,64,2048]{2,1,0:T(8,128)(2,1)} async-done(((bf16[4,64,2048]{2,1,0:T(8,128)(2,1)}), bf16[4,64,2048]{2,1,0:T(8,128)(2,1)}, u32[]{:S(2)}, u32[]{:S(2)}) %all-to-all-start.2) | async-done | bytes 1048608 | tf_op jit(solution)/shard_map/all_to_all | solution.py:42
  225.2 7.8 %conditional.10 = (bf16[128,2048]{1,0:T(8,128)(2,1)}, bf16[64,2048]{1,0:T(8,128)(2,1)}, f32[2048]{0:T(1024)S(1)}, bf16[2048,3072]{0,1:T(8,128)(2,1)}) conditional(s32[]{:T(128)} %convert_element_type.210, () %tuple.81, (bf16[128,2048]{1,0:T(8,128)(2,1)S(1)}, bf16[128,3072]{0,1:T(8,128)(2,1)}, bf16[4,64,2048]{2,1,0:T(8,128)(2,1)}, ...), branch_computations={%region_13.0_spmd, %region_14.20_spmd} | conditional | flops 4313053184 | bytes 156054880 | solution.py:106
  226.8 6.1 broadcast.189.clone
  234.3 124.3 %collective-permute-done.1 = bf16[64,2048]{1,0:T(8,128)(2,1)S(1)} collective-permute-done((bf16[64,2048]{1,0:T(8,128)(2,1)}, bf16[64,2048]{1,0:T(8,128)(2,1)S(1)}, u32[]{:S(2)}, u32[]{:S(2)}) %collective-permute-start.1) | collective-permute-done | bytes 262176 | tf_op jit(solution)/shard_map/ppermute | solution.py:31
  358.7 15.2 %conditional.11 = (bf16[1024,2048]{1,0:T(8,128)(2,1)}, bf16[64,1024]{1,0:T(8,128)(2,1)S(1)}, f32[8,64,1]{1,0,2:T(8,128)}, bf16[64,1024]{1,0:T(8,128)(2,1)S(1)}) conditional(s32[]{:T(128)} %convert_element_type.206, () %tuple.78, (bf16[64,1024]{1,0:T(8,128)(2,1)}, bf16[64,2048]{1,0:T(8,128)(2,1)S(1)}, bf16[1024,2048]{1,0:T(8,128)(2,1)}, ...), branch_computations={%region_20.21_spmd, %region_21.23_spmd} | conditional | flops 674889216 | bytes 42209396 | solution.py:106
  369.7 4.2 convolution_convert_fusion.5
  375.5 4.7 broadcast_select_fusion.1
  381.1 7.2 %all_gather.21 = f32[24,256,1]{0,2,1:T(1,128)S(1)} all-gather(f32[24,64,1]{0,2,1:T(1,128)S(1)} %copy.324), channel_id=1, replica_groups=mesh['section'=2,'render'=4,'dp'=16] {'render'}, dimensions={1}, use_global_device_ids=true | all-gather | bytes 30720 | tf_op jit(solution)/shard_map/all_gather | solution.py:49
  388.3 6.6 all-gather.8.cloned.1.call-done
  394.9 8.9 %conditional.12 = (bf16[128,2048]{0,1:T(8,128)(2,1)S(1)}) conditional(s32[]{:T(128)} %convert_element_type.206, () %tuple.88, (bf16[256,2048]{1,0:T(8,128)(2,1)}, bf16[128,2048]{1,0:T(8,128)(2,1)S(1)}, f32[24,256,1]{0,2,1:T(1,128)S(1)}) %tuple.191), branch_computations={%region_23.24_spmd, %region_24.0_spmd} | conditional | flops 271843328 | bytes 13754376 | solution.py:106
  403.8 32.5 %conditional.13 = (bf16[2048,3072]{0,1:T(8,128)(2,1)}, bf16[128,2048]{1,0:T(8,128)(2,1)}, f32[2048]{0:T(1024)S(1)}) conditional(s32[]{:T(128)} %convert_element_type.206, () %tuple.77, (bf16[128,2048]{1,0:T(8,128)(2,1)S(1)}, bf16[64,1024]{1,0:T(8,128)(2,1)S(1)}, bf16[128,2048]{0,1:T(8,128)(2,1)S(1)}, f32[128,1]{0,1:T(1,128)}, ...), branch_computations={%region_25.0_spmd, %region_26.29_spmd} | conditional | flops 2721184000 | bytes 65828460 | solution.py:106
  405.5 7.2 %fusion.101 = f32[128,2048]{1,0:T(8,128)S(1)} fusion(bf16[128,2048]{0,1:T(8,128)(2,1)} %copy-done.8, bf16[2048,3072]{1,0:T(8,128)(2,1)} %get-tuple-element.182), kind=kOutput, calls=%fused_computation.122 | convolution fusion | flops 1073741824 | bytes 9961472 | tf_op jit(solution)/shard_map/cond/branch_1_fun/nc,dc->nd/dot_general | solution.py:331
  421.7 14.6 %pad_maximum_fusion.5 = bf16[2048,3072]{0,1:T(8,128)(2,1)} fusion(bf16[2048,2048]{0,1:T(8,128)(2,1)S(1)} %convolution_convert_fusion.9, bf16[2048,1024]{0,1:T(8,128)(2,1)S(1)} %convolution_convert_fusion.10), kind=kLoop, calls=%fused_computation.121 | loop fusion | flops 25165824 | bytes 25165824 | tf_op jit(solution)/shard_map/cond/branch_1_fun/concatenate | solution.py:330
  436.3 10.7 %broadcast_select_fusion = bf16[2048,3072]{0,1:T(8,128)(2,1)} fusion(bf16[2048,3072]{0,1:T(8,128)(2,1)} %get-tuple-element.228, bf16[2048,3072]{0,1:T(8,128)(2,1)} %get-tuple-element.472, pred[]{:T(512)S(6)} %eq.3), kind=kLoop, calls=%fused_computation.146 | loop fusion | flops 6291456 | bytes 37748736 | tf_op jit(solution)/shard_map/jit(_where)/select_n | solution.py:344
  449.7 110.1 %reduce-scatter.4.cloned.1.call-done = bf16[2048,768]{0,1:T(8,128)(2,1)} async-done(((bf16[2048,3072]{0,1:T(8,128)(2,1)}), bf16[2048,768]{0,1:T(8,128)(2,1)}) %reduce-scatter.4.cloned.1.call-update) | async-done | bytes 3145744 | tf_op jit(solution)/shard_map/reduce_scatter | solution.py:348
  565.6 4.4 pad_maximum_fusion.6
  570.0 4.9 reshape.278
  574.9 76.6 %reduce-scatter.8.cloned.1.call-done = bf16[1024,128]{1,0:T(8,128)(2,1)} async-done(((bf16[16384,128]{1,0:T(8,128)(2,1)}), bf16[1024,128]{1,0:T(8,128)(2,1)}) %reduce-scatter.8.cloned.1.call-update) | async-done | bytes 262160 | tf_op jit(solution)/shard_map/reduce_scatter | solution.py:59
  655.2 8.7 %all-to-all-start.3 = ((f32[64,1,2048]{2,1,0:T(1,128)}), f32[64,1,2048]{2,1,0:T(1,128)S(1)}, u32[]{:S(2)}, u32[]{:S(2)}) async-start(f32[64,1,2048]{2,1,0:T(1,128)} %broadcast_in_dim.29), calls=%async_computation.6 | async-start | bytes 1048576 | tf_op jit(solution)/shard_map/all_to_all | solution.py:19
  665.8 10.2 %all-to-all-done.3 = f32[64,1,2048]{2,1,0:T(1,128)S(1)} async-done(((f32[64,1,2048]{2,1,0:T(1,128)}), f32[64,1,2048]{2,1,0:T(1,128)S(1)}, u32[]{:S(2)}, u32[]{:S(2)}) %all-to-all-start.3) | async-done | bytes 524320 | tf_op jit(solution)/shard_map/all_to_all | solution.py:19
  677.0 4.5 all-gather.14.cloned.1.call-done
  (121 shorter events, 90.6 us)
Async XLA Ops:
  7.2 96.1 %all-gather.10.cloned.1.call-start = ((), (), s32[]{:S(2)}) async-start(), calls=%async_computation.11 | async-start | bytes 13369344 | tf_op jit(solution)/shard_map/all_gather | solution.py:198
  7.9 148.6 %all-gather.12.cloned.1.call-start = ((), (), s32[]{:S(2)}) async-start(), calls=%async_computation.12 | async-start | bytes 4456448 | tf_op jit(solution)/shard_map/all_gather | solution.py:199
  9.9 215.3 %copy-start.19 = (f32[128,1]{0,1:T(1,128)}, f32[128,1]{0,1:T(1,128)S(1)}, u32[]{:S(2)}) copy-start(f32[128,1]{0,1:T(1,128)S(1)} %get-tuple-element.506) | copy-start | bytes 1540
  109.6 7.1 %copy-start.3 = (bf16[128,3072]{1,0:T(8,128)(2,1)}, bf16[128,3072]{1,0:T(8,128)(2,1)S(1)}, u32[]{:S(2)}) copy-start(bf16[128,3072]{1,0:T(8,128)(2,1)S(1)} %convolution_convert_fusion.11) | copy-start | bytes 2359300
  109.7 1.9 copy-start.6
  111.6 30.0 %all-to-all-start = ((bf16[4,128,2048]{1,2,0:T(8,128)(2,1)}), bf16[4,128,2048]{1,2,0:T(8,128)(2,1)}, u32[]{:S(2)}, u32[]{:S(2)}) async-start(bf16[4,128,2048]{1,2,0:T(8,128)(2,1)} %broadcast_in_dim.22), calls=%async_computation | async-start | bytes 4194304 | tf_op jit(solution)/shard_map/all_to_all | solution.py:19
  116.7 39.8 %copy-start.2 = (bf16[1,1,128,2048]{3,2,1,0:T(8,128)(2,1)S(1)}, bf16[1,1,128,2048]{3,2,1,0:T(8,128)(2,1)}, u32[]{:S(2)}) copy-start(bf16[1,1,128,2048]{3,2,1,0:T(8,128)(2,1)} %param.25) | copy-start | bytes 1572868
  156.5 21.5 %copy-start.14 = (f32[1,2048]{1,0:T(1,128)S(1)}, f32[1,2048]{1,0:T(1,128)}, u32[]{:S(2)}) copy-start(f32[1,2048]{1,0:T(1,128)} %param.28) | copy-start | bytes 24580
  162.6 6.1 copy-start
  170.5 0.7 copy-start.15
  171.2 6.9 collective-permute-start
  179.9 19.1 %all-to-all-start.1 = ((bf16[4,64,2048]{2,1,0:T(8,128)(2,1)}), bf16[4,64,2048]{2,1,0:T(8,128)(2,1)}, u32[]{:S(2)}, u32[]{:S(2)}) async-start(bf16[4,64,2048]{2,1,0:T(8,128)(2,1)} %broadcast_in_dim.25), calls=%async_computation.1 | async-start | bytes 2097152 | tf_op jit(solution)/shard_map/all_to_all | solution.py:19
  206.4 18.8 %all-to-all-start.2 = ((bf16[4,64,2048]{2,1,0:T(8,128)(2,1)}), bf16[4,64,2048]{2,1,0:T(8,128)(2,1)}, u32[]{:S(2)}, u32[]{:S(2)}) async-start(bf16[4,64,2048]{2,1,0:T(8,128)(2,1)} %bitcast.193), calls=%async_computation.2 | async-start | bytes 2097152 | tf_op jit(solution)/shard_map/all_to_all | solution.py:42
  211.5 183.4 %all-gather.8.cloned.1.call-start = ((), (), s32[]{:S(2)}) async-start(), calls=%async_computation.7 | async-start | bytes 1310720 | tf_op jit(solution)/shard_map/all_gather | solution.py:49
  233.0 125.6 %copy-start.17 = (f32[2048]{0:T(1024)}, f32[2048]{0:T(1024)S(1)}, u32[]{:S(2)}) copy-start(f32[2048]{0:T(1024)S(1)} %get-tuple-element.233) | copy-start | bytes 24580
  233.0 125.6 %collective-permute-start.1 = (bf16[64,2048]{1,0:T(8,128)(2,1)}, bf16[64,2048]{1,0:T(8,128)(2,1)S(1)}, u32[]{:S(2)}, u32[]{:S(2)}) collective-permute-start(bf16[64,2048]{1,0:T(8,128)(2,1)} %get-tuple-element.219), channel_id=1, source_target_pairs={{64,0},{65,1},{66,2},{67,3},{68,4},{69,5},{70,6},{71,7},{72,8},{73... | collective-permute-start | bytes 786440 | tf_op jit(solution)/shard_map/ppermute | solution.py:31
  361.4 2.8 copy-start.1
  365.6 4.0 copy-start.11
  369.6 4.2 copy-start.12
  375.5 71.9 %reduce-scatter.6.cloned.1.call-start = ((), (), s32[]{:S(2)}) async-start(), calls=%async_computation.9 | async-start | bytes 5242880 | tf_op jit(solution)/shard_map/reduce_scatter | solution.py:351
  380.2 14.7 %copy-start.7 = (bf16[128,2048]{1,0:T(8,128)(2,1)S(1)}, bf16[128,2048]{1,0:T(8,128)(2,1)}, u32[]{:S(2)}) copy-start(bf16[128,2048]{1,0:T(8,128)(2,1)} %copy-done.6) | copy-start | bytes 1572868
  380.2 179.5 %reduce-scatter.4.cloned.1.call-start = ((), (), s32[]{:S(2)}) async-start(), calls=%async_computation.8 | async-start | bytes 15728640 | tf_op jit(solution)/shard_map/reduce_scatter | solution.py:348
  404.1 0.8 copy-start.8
  412.7 3.6 copy-start.20
  418.0 1.3 copy-start.9
  447.0 204.6 %reduce-scatter.8.cloned.1.call-start = ((), (), s32[]{:S(2)}) async-start(), calls=%async_computation.10 | async-start | bytes 4456448 | tf_op jit(solution)/shard_map/reduce_scatter | solution.py:59
  574.9 79.2 %copy-start.18 = (f32[2048]{0:T(1024)S(1)}, f32[2048]{0:T(1024)}, u32[]{:S(2)}) copy-start(f32[2048]{0:T(1024)} %copy-done.17) | copy-start | bytes 24580
  574.9 106.6 %all-gather.14.cloned.1.call-start = ((), (), s32[]{:S(2)}) async-start(), calls=%async_computation.13 | async-start | bytes 1310720 | tf_op jit(solution)/shard_map/all_gather | solution.py:69
  655.2 20.8 %all-to-all-start.3 = ((f32[64,1,2048]{2,1,0:T(1,128)}), f32[64,1,2048]{2,1,0:T(1,128)S(1)}, u32[]{:S(2)}, u32[]{:S(2)}) async-start(f32[64,1,2048]{2,1,0:T(1,128)} %broadcast_in_dim.29), calls=%async_computation.6 | async-start | bytes 1048576 | tf_op jit(solution)/shard_map/all_to_all | solution.py:19
Sparse Core Ops, SparseCore 0:
  10.1 93.0 all-gather.9
  105.4 51.1 all-gather.11
  375.6 19.2 all-gather.7
  397.2 46.0 reduce-scatter.5
  447.1 112.6 reduce-scatter.3
  575.0 76.4 reduce-scatter.7
  654.2 27.2 all-gather.13
where the time goes:
time: 702 us; the launch traced here: 694 us
  waiting for transfers between devices  495 us (71%)
  local copies, waits for them, and re-layouts  58 us (8%)
  other arithmetic  50.1 us (7%)
  matrix products  40.3 us (6%)
  starting transfers between devices  27.4 us (4%)
  between operations  14.8 us (2%)
  blocking collectives  7.17 us (1%)
    ppermute x2, waiting for transfers between devices, shifted(): return lax.ppermute(block, axis, route)  130 us
    reduce_scatter x1, waiting for transfers between devices, shards(): lax.psum_scatter(qkv_part.astype(jnp.bfloat16), 'render', scatter_dimensi...  110 us
    all_gather x1, waiting for transfers between devices, shards(): lax.all_gather(w_qkv[0], 'dp', axis=0, tiled=True)  92.1 us
    reduce_scatter x1, waiting for transfers between devices, sum_packed(): lax.psum_scatter(lines, axis, tiled=True).reshape(-1)  76.6 us
    all_to_all x3, waiting for transfers between devices, sent_to_all(): lax.all_to_all(jnp.broadcast_to(shard[None], (peers, *shard.shape)), axis...  48.2 us
    another operation x15, local copies, waits for them, and re-layouts  19.8 us
    all_to_all x3, starting transfers between devices, sent_to_all(): lax.all_to_all(jnp.broadcast_to(shard[None], (peers, *shard.shape)), axis...  19.2 us
    concatenate x1, other arithmetic, encoder_finish(): jnp.concatenate([query_weight_part, key_weight_part], 1)  14.6 us
  transfers between devices with their start and end apart: 13, of which 12 were waited for; matrix products, arithmetic and copies ran while one was open for 11% of the time, Pallas kernels for 0%

commit v1 on v0

--- a/solution.py
+++ b/solution.py
@@ -6,6 +6,22 @@
 HEADS = 8
 HD = 128
 NORM_EPSILON = 1e-06
+
+
+def ring_gather(x, axis, dim):
+    ways, here, step = (lax.axis_size(axis), lax.axis_index(axis), x.shape[dim])
+    shape = [n * ways if d == dim else n for d, n in enumerate(x.shape)]
+    full = lax.dynamic_update_slice_in_dim(jnp.zeros(shape, x.dtype), x, here * step, axis=dim)
+    going_up = going_down = x
+    for far in range(1, ways // 2 + 1):
+        going_up = lax.ppermute(going_up, axis, [(d, (d + 1) % ways) for d in range(ways)])
+        full = lax.dynamic_update_slice_in_dim(full, going_up, (here - far) % ways * step, axis=dim)
+        if 2 * far < ways:
+            going_down = lax.ppermute(going_down, axis, [(d, (d - 1) % ways) for d in range(ways)])
+            full = lax.dynamic_update_slice_in_dim(
+                full, going_down, (here + far) % ways * step, axis=dim
+            )
+    return full
 
 
 def joined_along(blocks, dim):
@@ -195,7 +211,7 @@
     is_encoder = section_index == 0
     is_decoder = jnp.logical_not(is_encoder)
     full_qkv, full_out = (
-        lax.all_gather(w_qkv[0], "dp", axis=0, tiled=True),
+        ring_gather(w_qkv[0], "dp", 0),
         lax.all_gather(w_out[0], "dp", axis=0, tiled=True),
     )
     normed, row_scale = rms_norm(tokens, gain_row)

time: 702 us -> 775 us (1.10)
  starting transfers between devices: 27.4 us -> 77.5 us
  local copies, waits for them, and re-layouts: 58 us -> 84.9 us
    ppermute x0 -> x15, waiting for transfers between devices: none -> 104 us  [the longest x8 89 us: ring_gather(): lax.ppermute(going_up, axis, [(d, (d + 1) % ways) for d in range(ways)])]
    all_gather x1 -> x0, waiting for transfers between devices: 92.1 us -> none  [shards(): lax.all_gather(w_qkv[0], 'dp', axis=0, tiled=True)]
    ppermute x0 -> x15, starting transfers between devices: none -> 36.9 us  [the longest x7 34.8 us: ring_gather(): lax.ppermute(going_down, axis, [(d, (d - 1) % ways) for d in range(ways)])]
    dynamic_update_slice x0 -> x16, local copies, waits for them, and re-layouts: none -> 20.9 us  [the longest x8 11 us: ring_gather(): lax.dynamic_update_slice_in_dim(full, going_up, (here - far) % ways * ste...]
    all_to_all x3, starting transfers between devices: 19.2 us -> 32.4 us  [sent_to_all(): lax.all_to_all(jnp.broadcast_to(shard[None], (peers, *shard.shape)), axis...]
    all_gather x1, waiting for transfers between devices: 12 us -> 0.02 us  [shards(): lax.all_gather(w_out[0], 'dp', axis=0, tiled=True)]
    another operation x15 -> x16, local copies, waits for them, and re-layouts: 19.8 us -> 25.9 us
  transfers between devices with their start and end apart: 13 -> 27, of which waited for: 12 -> 23; matrix products, arithmetic and copies ran while one was open for 11% -> 14% of each run, Pallas kernels for 0% -> 0%
where the time goes in v1:
time: 775 us; the launch traced here: 765 us
  waiting for transfers between devices  489 us (63%)
  local copies, waits for them, and re-layouts  84.9 us (11%)
  starting transfers between devices  77.5 us (10%)
  other arithmetic  49.3 us (6%)
  matrix products  41 us (5%)
  between operations  14.9 us (2%)
    ppermute x2, waiting for transfers between devices, shifted(): return lax.ppermute(block, axis, route)  130 us
    reduce_scatter x1, waiting for transfers between devices, shards(): lax.psum_scatter(qkv_part.astype(jnp.bfloat16), 'render', scatter_dimensi...  110 us
    ppermute x8, waiting for transfers between devices, ring_gather(): lax.ppermute(going_up, axis, [(d, (d + 1) % ways) for d in range(ways)])  89 us
    reduce_scatter x1, waiting for transfers between devices, sum_packed(): lax.psum_scatter(lines, axis, tiled=True).reshape(-1)  76.7 us
    all_to_all x3, waiting for transfers between devices, sent_to_all(): lax.all_to_all(jnp.broadcast_to(shard[None], (peers, *shard.shape)), axis...  47.1 us
    ppermute x7, starting transfers between devices, ring_gather(): lax.ppermute(going_down, axis, [(d, (d - 1) % ways) for d in range(ways)])  34.8 us
    all_to_all x3, starting transfers between devices, sent_to_all(): lax.all_to_all(jnp.broadcast_to(shard[None], (peers, *shard.shape)), axis...  32.4 us
    another operation x16, local copies, waits for them, and re-layouts  25.9 us
  transfers between devices with their start and end apart: 27, of which 23 were waited for; matrix products, arithmetic and copies ran while one was open for 14% of the time, Pallas kernels for 0%

profile of v1, /device:TPU:1, one launch (start us, length us, event | category | flops | bytes accessed | tf_op | source)
XLA Modules:
  0.0 764.8 jit_solution(290428028269016351)
XLA Ops:
  13.1 17.3 %collective-permute-done = bf16[128,3072]{1,0:T(8,128)(2,1)S(1)} collective-permute-done((bf16[128,3072]{1,0:T(8,128)(2,1)}, bf16[128,3072]{1,0:T(8,128)(2,1)S(1)}, u32[]{:S(2)}, u32[]{:S(2)}) %collective-permute-start) | collective-permute-done | bytes 786464 | tf_op jit(solution)/shard_map/ppermute | solution.py:17
  36.6 16.7 %collective-permute-done.2 = bf16[128,3072]{1,0:T(8,128)(2,1)S(1)} collective-permute-done((bf16[128,3072]{1,0:T(8,128)(2,1)S(1)}, bf16[128,3072]{1,0:T(8,128)(2,1)S(1)}, u32[]{:S(2)}, u32[]{:S(2)}) %collective-permute-start.2) | collective-permute-done | bytes 786464 | tf_op jit(solution)/shard_map/ppermute | solution.py:17
  53.3 6.1 broadcast.217
  65.1 8.9 %collective-permute-done.4 = bf16[128,3072]{1,0:T(8,128)(2,1)} collective-permute-done((bf16[128,3072]{1,0:T(8,128)(2,1)S(1)}, bf16[128,3072]{1,0:T(8,128)(2,1)}, u32[]{:S(2)}, u32[]{:S(2)}) %collective-permute-start.4) | collective-permute-done | bytes 786464 | tf_op jit(solution)/shard_map/ppermute | solution.py:17
  78.5 5.5 collective-permute-start.7
  84.9 16.2 %collective-permute-done.6 = bf16[128,3072]{1,0:T(8,128)(2,1)} collective-permute-done((bf16[128,3072]{1,0:T(8,128)(2,1)}, bf16[128,3072]{1,0:T(8,128)(2,1)}, u32[]{:S(2)}, u32[]{:S(2)}) %collective-permute-start.6) | collective-permute-done | bytes 786464 | tf_op jit(solution)/shard_map/ppermute | solution.py:17
  104.3 7.5 collective-permute-done.7
  111.8 5.4 collective-permute-start.9
  127.4 5.5 collective-permute-start.11
  149.1 7.9 %collective-permute-done.12 = bf16[128,3072]{1,0:T(8,128)(2,1)S(1)} collective-permute-done((bf16[128,3072]{1,0:T(8,128)(2,1)S(1)}, bf16[128,3072]{1,0:T(8,128)(2,1)S(1)}, u32[]{:S(2)}, u32[]{:S(2)}) %collective-permute-start.12) | collective-permute-done | bytes 786464 | tf_op jit(solution)/shard_map/ppermute | solution.py:17
  162.0 14.1 %collective-permute-done.14 = bf16[128,3072]{1,0:T(8,128)(2,1)S(1)} collective-permute-done((bf16[128,3072]{1,0:T(8,128)(2,1)S(1)}, bf16[128,3072]{1,0:T(8,128)(2,1)S(1)}, u32[]{:S(2)}, u32[]{:S(2)}) %collective-permute-start.14) | collective-permute-done | bytes 786464 | tf_op jit(solution)/shard_map/ppermute | solution.py:17
  177.0 6.4 convolution_convert_fusion.11
  185.4 16.9 %all-to-all-start = ((bf16[4,128,2048]{1,2,0:T(8,128)(2,1)}), bf16[4,128,2048]{1,2,0:T(8,128)(2,1)}, u32[]{:S(2)}, u32[]{:S(2)}) async-start(bf16[4,128,2048]{1,2,0:T(8,128)(2,1)} %broadcast_in_dim.22), calls=%async_computation | async-start | bytes 4194304 | tf_op jit(solution)/shard_map/all_to_all | solution.py:35
  202.9 23.2 %all-to-all-done = bf16[4,128,2048]{1,2,0:T(8,128)(2,1)} async-done(((bf16[4,128,2048]{1,2,0:T(8,128)(2,1)}), bf16[4,128,2048]{1,2,0:T(8,128)(2,1)}, u32[]{:S(2)}, u32[]{:S(2)}) %all-to-all-start) | async-done | bytes 2097184 | tf_op jit(solution)/shard_map/all_to_all | solution.py:35
  229.1 14.1 %conditional.7 = (bf16[64,1024]{1,0:T(8,128)(2,1)}, f32[8,64,512]{2,1,0:T(8,128)}, f32[8,64,1]{1,0,2:T(8,128)}, f32[8,64,1]{1,0,2:T(8,128)}, bf16[64,2048]{1,0:T(8,128)(2,1)S(1)}) conditional(s32[]{:T(128)} %convert_element_type.196, () %tuple.76, (bf16[64,1024]{1,0:T(8,128)(2,1)}, bf16[512,2048]{1,0:T(8,128)(2,1)S(1)}, ...), branch_computations={%region_1.2_spmd, %region_2.5_spmd} | conditional | flops 404945920 | bytes 37890116 | solution.py:122
  251.3 6.8 all-to-all-start.1
  258.1 13.7 %all-to-all-done.1 = bf16[4,64,2048]{2,1,0:T(8,128)(2,1)} async-done(((bf16[4,64,2048]{2,1,0:T(8,128)(2,1)}), bf16[4,64,2048]{2,1,0:T(8,128)(2,1)}, u32[]{:S(2)}, u32[]{:S(2)}) %all-to-all-start.1) | async-done | bytes 1048608 | tf_op jit(solution)/shard_map/all_to_all | solution.py:35
  283.7 13.7 %all-to-all-done.2 = bf16[4,64,2048]{2,1,0:T(8,128)(2,1)} async-done(((bf16[4,64,2048]{2,1,0:T(8,128)(2,1)}), bf16[4,64,2048]{2,1,0:T(8,128)(2,1)}, u32[]{:S(2)}, u32[]{:S(2)}) %all-to-all-start.2) | async-done | bytes 1048608 | tf_op jit(solution)/shard_map/all_to_all | solution.py:58
  297.4 7.9 %conditional.10 = (bf16[128,2048]{1,0:T(8,128)(2,1)}, bf16[64,2048]{1,0:T(8,128)(2,1)}, f32[2048]{0:T(1024)S(1)}, bf16[2048,3072]{0,1:T(8,128)(2,1)}) conditional(s32[]{:T(128)} %convert_element_type.200, () %tuple.78, (bf16[128,2048]{1,0:T(8,128)(2,1)S(1)}, bf16[128,3072]{0,1:T(8,128)(2,1)}, bf16[4,64,2048]{2,1,0:T(8,128)(2,1)}, ...), branch_computations={%region_13.14_spmd, %region_14.20_spmd} | conditional | flops 4313053184 | bytes 156054880 | solution.py:122
  299.0 6.1 broadcast.200.clone
  306.6 125.6 %collective-permute-done.16 = bf16[64,2048]{1,0:T(8,128)(2,1)S(1)} collective-permute-done((bf16[64,2048]{1,0:T(8,128)(2,1)}, bf16[64,2048]{1,0:T(8,128)(2,1)S(1)}, u32[]{:S(2)}, u32[]{:S(2)}) %collective-permute-start.16) | collective-permute-done | bytes 262176 | tf_op jit(solution)/shard_map/ppermute | solution.py:47
  432.2 16.0 %conditional.11 = (bf16[1024,2048]{1,0:T(8,128)(2,1)}, bf16[64,1024]{1,0:T(8,128)(2,1)}, f32[8,64,1]{1,0,2:T(8,128)}, bf16[64,1024]{1,0:T(8,128)(2,1)S(1)}) conditional(s32[]{:T(128)} %convert_element_type.196, () %tuple.75, (bf16[64,1024]{1,0:T(8,128)(2,1)}, bf16[64,2048]{1,0:T(8,128)(2,1)S(1)}, bf16[1024,2048]{1,0:T(8,128)(2,1)}, ...), branch_computations={%region_20.21_spmd, %region_21.23_spmd} | conditional | flops 674889216 | bytes 41160764 | solution.py:122
  455.5 7.4 all_gather.17
  465.8 8.9 %conditional.12 = (bf16[128,2048]{0,1:T(8,128)(2,1)S(1)}) conditional(s32[]{:T(128)} %convert_element_type.196, () %tuple.85, (bf16[256,2048]{1,0:T(8,128)(2,1)}, bf16[128,2048]{1,0:T(8,128)(2,1)S(1)}, f32[24,256,1]{0,2,1:T(1,128)S(1)}) %tuple.183), branch_computations={%region_23.24_spmd, %region_24.25_spmd} | conditional | flops 271843328 | bytes 13754376 | solution.py:122
  474.7 32.4 %conditional.13 = (bf16[2048,3072]{0,1:T(8,128)(2,1)}, bf16[128,2048]{1,0:T(8,128)(2,1)}, f32[2048]{0:T(1024)S(1)}) conditional(s32[]{:T(128)} %convert_element_type.196, () %tuple.74, (bf16[128,2048]{1,0:T(8,128)(2,1)S(1)}, bf16[64,1024]{1,0:T(8,128)(2,1)S(1)}, bf16[128,2048]{0,1:T(8,128)(2,1)S(1)}, f32[128,1]{0,1:T(1,128)}, ...), branch_computations={%region_25.26_spmd, %region_26.0_spmd} | conditional | flops 2721184000 | bytes 65828460 | solution.py:122
  476.4 7.2 fusion.101
  492.5 14.6 %pad_maximum_fusion.5 = bf16[2048,3072]{0,1:T(8,128)(2,1)} fusion(bf16[2048,2048]{0,1:T(8,128)(2,1)S(1)} %convolution_convert_fusion.9, bf16[2048,1024]{0,1:T(8,128)(2,1)S(1)} %convolution_convert_fusion.10), kind=kLoop, calls=%fused_computation.121 | loop fusion | flops 25165824 | bytes 25165824 | tf_op jit(solution)/shard_map/cond/branch_1_fun/concatenate | solution.py:346
  507.1 10.7 %broadcast_select_fusion = bf16[2048,3072]{0,1:T(8,128)(2,1)} fusion(bf16[2048,3072]{0,1:T(8,128)(2,1)} %get-tuple-element.206, bf16[2048,3072]{0,1:T(8,128)(2,1)} %get-tuple-element.450, pred[]{:T(512)S(6)} %eq.19), kind=kLoop, calls=%fused_computation.146 | loop fusion | flops 6291456 | bytes 37748736 | tf_op jit(solution)/shard_map/jit(_where)/select_n | solution.py:360
  520.5 110.1 %reduce-scatter.4.cloned.1.call-done = bf16[2048,768]{0,1:T(8,128)(2,1)} async-done(((bf16[2048,3072]{0,1:T(8,128)(2,1)}), bf16[2048,768]{0,1:T(8,128)(2,1)}) %reduce-scatter.4.cloned.1.call-update) | async-done | bytes 3145744 | tf_op jit(solution)/shard_map/reduce_scatter | solution.py:364
  645.8 76.7 %reduce-scatter.8.cloned.1.call-done = bf16[1024,128]{1,0:T(8,128)(2,1)} async-done(((bf16[16384,128]{1,0:T(8,128)(2,1)}), bf16[1024,128]{1,0:T(8,128)(2,1)}) %reduce-scatter.8.cloned.1.call-update) | async-done | bytes 262160 | tf_op jit(solution)/shard_map/reduce_scatter | solution.py:75
  726.0 8.7 %all-to-all-start.3 = ((f32[64,1,2048]{2,1,0:T(1,128)}), f32[64,1,2048]{2,1,0:T(1,128)S(1)}, u32[]{:S(2)}, u32[]{:S(2)}) async-start(f32[64,1,2048]{2,1,0:T(1,128)} %broadcast_in_dim.29), calls=%async_computation.6 | async-start | bytes 1048576 | tf_op jit(solution)/shard_map/all_to_all | solution.py:35
  736.7 10.2 %all-to-all-done.3 = f32[64,1,2048]{2,1,0:T(1,128)S(1)} async-done(((f32[64,1,2048]{2,1,0:T(1,128)}), f32[64,1,2048]{2,1,0:T(1,128)S(1)}, u32[]{:S(2)}, u32[]{:S(2)}) %all-to-all-start.3) | async-done | bytes 524320 | tf_op jit(solution)/shard_map/all_to_all | solution.py:35
  (165 shorter events, 185.1 us)
Async XLA Ops:
  7.2 221.9 %all-gather.8.cloned.1.call-start = ((), (), s32[]{:S(2)}) async-start(), calls=%async_computation.11 | async-start | bytes 4456448 | tf_op jit(solution)/shard_map/all_gather | solution.py:215
  7.2 23.3 %collective-permute-start = (bf16[128,3072]{1,0:T(8,128)(2,1)}, bf16[128,3072]{1,0:T(8,128)(2,1)S(1)}, u32[]{:S(2)}, u32[]{:S(2)}) collective-permute-start(bf16[128,3072]{1,0:T(8,128)(2,1)} %bitcast.212), channel_id=1, source_target_pairs={{0,1},{1,2},{2,3},{3,4},{4,5},{5,6},{6,7},{7,8},{8,9},{9,10},{10,1... | collective-permute-start | bytes 2359304 | tf_op jit(solution)/shard_map/ppermute | solution.py:17
  9.3 22.7 %collective-permute-start.1 = (bf16[128,3072]{1,0:T(8,128)(2,1)}, bf16[128,3072]{1,0:T(8,128)(2,1)S(1)}, u32[]{:S(2)}, u32[]{:S(2)}) collective-permute-start(bf16[128,3072]{1,0:T(8,128)(2,1)} %bitcast.213), channel_id=1, source_target_pairs={{0,15},{1,0},{2,1},{3,2},{4,3},{5,4},{6,5},{7,6},{8,7},{9,8},{10,9... | collective-permute-start | bytes 2359304 | tf_op jit(solution)/shard_map/ppermute | solution.py:20
  30.5 28.9 %copy-start.13 = (bf16[128,3072]{1,0:T(8,128)(2,1)}, bf16[128,3072]{1,0:T(8,128)(2,1)S(1)}, u32[]{:S(2)}) copy-start(bf16[128,3072]{1,0:T(8,128)(2,1)S(1)} %collective-permute-done) | copy-start | bytes 2359300
  30.5 22.8 %collective-permute-start.2 = (bf16[128,3072]{1,0:T(8,128)(2,1)S(1)}, bf16[128,3072]{1,0:T(8,128)(2,1)S(1)}, u32[]{:S(2)}, u32[]{:S(2)}) collective-permute-start(bf16[128,3072]{1,0:T(8,128)(2,1)S(1)} %collective-permute-done), channel_id=1, source_target_pairs={{0,1},{1,2},{2,3},{3,4},{4,5},{5,6},{6,7},{7,8},{8,9},{9,10},{10,1... | collective-permute-start | bytes 2359304 | tf_op jit(solution)/shard_map/ppermute | solution.py:17
  32.0 28.4 %collective-permute-start.3 = (bf16[128,3072]{1,0:T(8,128)(2,1)S(1)}, bf16[128,3072]{1,0:T(8,128)(2,1)}, u32[]{:S(2)}, u32[]{:S(2)}) collective-permute-start(bf16[128,3072]{1,0:T(8,128)(2,1)S(1)} %collective-permute-done.1), channel_id=1, source_target_pairs={{0,15},{1,0},{2,1},{3,2},{4,3},{5,4},{6,5},{7,6},{8,7},{9,8},{10,9... | collective-permute-start | bytes 2359304 | tf_op jit(solution)/shard_map/ppermute | solution.py:20
  53.3 20.7 %collective-permute-start.4 = (bf16[128,3072]{1,0:T(8,128)(2,1)S(1)}, bf16[128,3072]{1,0:T(8,128)(2,1)}, u32[]{:S(2)}, u32[]{:S(2)}) collective-permute-start(bf16[128,3072]{1,0:T(8,128)(2,1)S(1)} %collective-permute-done.2), channel_id=1, source_target_pairs={{0,1},{1,2},{2,3},{3,4},{4,5},{5,6},{6,7},{7,8},{8,9},{9,10},{10,1... | collective-permute-start | bytes 2359304 | tf_op jit(solution)/shard_map/ppermute | solution.py:17
  53.3 244.1 %copy-start.19 = (f32[128,1]{0,1:T(1,128)}, f32[128,1]{0,1:T(1,128)S(1)}, u32[]{:S(2)}) copy-start(f32[128,1]{0,1:T(1,128)S(1)} %get-tuple-element.484) | copy-start | bytes 1540
  53.3 20.7 %copy-start.2 = (bf16[1,1,128,2048]{3,2,1,0:T(8,128)(2,1)S(1)}, bf16[1,1,128,2048]{3,2,1,0:T(8,128)(2,1)}, u32[]{:S(2)}) copy-start(bf16[1,1,128,2048]{3,2,1,0:T(8,128)(2,1)} %param.25) | copy-start | bytes 1572868
  60.4 18.1 %collective-permute-start.5 = (bf16[128,3072]{1,0:T(8,128)(2,1)}, bf16[128,3072]{1,0:T(8,128)(2,1)}, u32[]{:S(2)}, u32[]{:S(2)}) collective-permute-start(bf16[128,3072]{1,0:T(8,128)(2,1)} %collective-permute-done.3), channel_id=1, source_target_pairs={{0,15},{1,0},{2,1},{3,2},{4,3},{5,4},{6,5},{7,6},{8,7},{9,8},{10,9... | collective-permute-start | bytes 2359304 | tf_op jit(solution)/shard_map/ppermute | solution.py:20
  74.0 27.1 %collective-permute-start.6 = (bf16[128,3072]{1,0:T(8,128)(2,1)}, bf16[128,3072]{1,0:T(8,128)(2,1)}, u32[]{:S(2)}, u32[]{:S(2)}) collective-permute-start(bf16[128,3072]{1,0:T(8,128)(2,1)} %collective-permute-done.4), channel_id=1, source_target_pairs={{0,1},{1,2},{2,3},{3,4},{4,5},{5,6},{6,7},{7,8},{8,9},{9,10},{10,1... | collective-permute-start | bytes 2359304 | tf_op jit(solution)/shard_map/ppermute | solution.py:17
  78.5 33.3 %collective-permute-start.7 = (bf16[128,3072]{1,0:T(8,128)(2,1)}, bf16[128,3072]{1,0:T(8,128)(2,1)S(1)}, u32[]{:S(2)}, u32[]{:S(2)}) collective-permute-start(bf16[128,3072]{1,0:T(8,128)(2,1)} %collective-permute-done.5), channel_id=1, source_target_pairs={{0,15},{1,0},{2,1},{3,2},{4,3},{5,4},{6,5},{7,6},{8,7},{9,8},{10,9... | collective-permute-start | bytes 2359304 | tf_op jit(solution)/shard_map/ppermute | solution.py:20
  101.1 20.9 %collective-permute-start.8 = (bf16[128,3072]{1,0:T(8,128)(2,1)}, bf16[128,3072]{1,0:T(8,128)(2,1)S(1)}, u32[]{:S(2)}, u32[]{:S(2)}) collective-permute-start(bf16[128,3072]{1,0:T(8,128)(2,1)} %collective-permute-done.6), channel_id=1, source_target_pairs={{0,1},{1,2},{2,3},{3,4},{4,5},{5,6},{6,7},{7,8},{8,9},{9,10},{10,1... | collective-permute-start | bytes 2359304 | tf_op jit(solution)/shard_map/ppermute | solution.py:17
  111.8 15.6 %collective-permute-start.9 = (bf16[128,3072]{1,0:T(8,128)(2,1)S(1)}, bf16[128,3072]{1,0:T(8,128)(2,1)S(1)}, u32[]{:S(2)}, u32[]{:S(2)}) collective-permute-start(bf16[128,3072]{1,0:T(8,128)(2,1)S(1)} %collective-permute-done.7), channel_id=1, source_target_pairs={{0,15},{1,0},{2,1},{3,2},{4,3},{5,4},{6,5},{7,6},{8,7},{9,8},{10,9... | collective-permute-start | bytes 2359304 | tf_op jit(solution)/shard_map/ppermute | solution.py:20
  122.1 16.9 %collective-permute-start.10 = (bf16[128,3072]{1,0:T(8,128)(2,1)S(1)}, bf16[128,3072]{1,0:T(8,128)(2,1)S(1)}, u32[]{:S(2)}, u32[]{:S(2)}) collective-permute-start(bf16[128,3072]{1,0:T(8,128)(2,1)S(1)} %collective-permute-done.8), channel_id=1, source_target_pairs={{0,1},{1,2},{2,3},{3,4},{4,5},{5,6},{6,7},{7,8},{8,9},{9,10},{10,1... | collective-permute-start | bytes 2359304 | tf_op jit(solution)/shard_map/ppermute | solution.py:17
  127.4 15.6 %collective-permute-start.11 = (bf16[128,3072]{1,0:T(8,128)(2,1)S(1)}, bf16[128,3072]{1,0:T(8,128)(2,1)S(1)}, u32[]{:S(2)}, u32[]{:S(2)}) collective-permute-start(bf16[128,3072]{1,0:T(8,128)(2,1)S(1)} %collective-permute-done.9), channel_id=1, source_target_pairs={{0,15},{1,0},{2,1},{3,2},{4,3},{5,4},{6,5},{7,6},{8,7},{9,8},{10,9... | collective-permute-start | bytes 2359304 | tf_op jit(solution)/shard_map/ppermute | solution.py:20
  139.0 18.0 %collective-permute-start.12 = (bf16[128,3072]{1,0:T(8,128)(2,1)S(1)}, bf16[128,3072]{1,0:T(8,128)(2,1)S(1)}, u32[]{:S(2)}, u32[]{:S(2)}) collective-permute-start(bf16[128,3072]{1,0:T(8,128)(2,1)S(1)} %collective-permute-done.10), channel_id=1, source_target_pairs={{0,1},{1,2},{2,3},{3,4},{4,5},{5,6},{6,7},{7,8},{8,9},{9,10},{10,1... | collective-permute-start | bytes 2359304 | tf_op jit(solution)/shard_map/ppermute | solution.py:17
  143.0 18.1 %collective-permute-start.13 = (bf16[128,3072]{1,0:T(8,128)(2,1)S(1)}, bf16[128,3072]{1,0:T(8,128)(2,1)S(1)}, u32[]{:S(2)}, u32[]{:S(2)}) collective-permute-start(bf16[128,3072]{1,0:T(8,128)(2,1)S(1)} %collective-permute-done.11), channel_id=1, source_target_pairs={{0,15},{1,0},{2,1},{3,2},{4,3},{5,4},{6,5},{7,6},{8,7},{9,8},{10,9... | collective-permute-start | bytes 2359304 | tf_op jit(solution)/shard_map/ppermute | solution.py:20
  157.0 19.1 %collective-permute-start.14 = (bf16[128,3072]{1,0:T(8,128)(2,1)S(1)}, bf16[128,3072]{1,0:T(8,128)(2,1)S(1)}, u32[]{:S(2)}, u32[]{:S(2)}) collective-permute-start(bf16[128,3072]{1,0:T(8,128)(2,1)S(1)} %collective-permute-done.12), channel_id=1, source_target_pairs={{0,1},{1,2},{2,3},{3,4},{4,5},{5,6},{6,7},{7,8},{8,9},{9,10},{10,1... | collective-permute-start | bytes 2359304 | tf_op jit(solution)/shard_map/ppermute | solution.py:17
  185.4 40.7 %all-to-all-start = ((bf16[4,128,2048]{1,2,0:T(8,128)(2,1)}), bf16[4,128,2048]{1,2,0:T(8,128)(2,1)}, u32[]{:S(2)}, u32[]{:S(2)}) async-start(bf16[4,128,2048]{1,2,0:T(8,128)(2,1)} %broadcast_in_dim.22), calls=%async_computation | async-start | bytes 4194304 | tf_op jit(solution)/shard_map/all_to_all | solution.py:35
  243.9 5.5 collective-permute-start.15
  251.3 20.5 %all-to-all-start.1 = ((bf16[4,64,2048]{2,1,0:T(8,128)(2,1)}), bf16[4,64,2048]{2,1,0:T(8,128)(2,1)}, u32[]{:S(2)}, u32[]{:S(2)}) async-start(bf16[4,64,2048]{2,1,0:T(8,128)(2,1)} %broadcast_in_dim.25), calls=%async_computation.1 | async-start | bytes 2097152 | tf_op jit(solution)/shard_map/all_to_all | solution.py:35
  278.6 18.8 %all-to-all-start.2 = ((bf16[4,64,2048]{2,1,0:T(8,128)(2,1)}), bf16[4,64,2048]{2,1,0:T(8,128)(2,1)}, u32[]{:S(2)}, u32[]{:S(2)}) async-start(bf16[4,64,2048]{2,1,0:T(8,128)(2,1)} %bitcast.190), calls=%async_computation.2 | async-start | bytes 2097152 | tf_op jit(solution)/shard_map/all_to_all | solution.py:58
  283.7 182.1 %all-gather.6.cloned.1.call-start = ((), (), s32[]{:S(2)}) async-start(), calls=%async_computation.7 | async-start | bytes 1310720 | tf_op jit(solution)/shard_map/all_gather | solution.py:65
  305.3 126.9 %copy-start.17 = (f32[2048]{0:T(1024)}, f32[2048]{0:T(1024)S(1)}, u32[]{:S(2)}) copy-start(f32[2048]{0:T(1024)S(1)} %get-tuple-element.211) | copy-start | bytes 24580
  305.3 126.9 %collective-permute-start.16 = (bf16[64,2048]{1,0:T(8,128)(2,1)}, bf16[64,2048]{1,0:T(8,128)(2,1)S(1)}, u32[]{:S(2)}, u32[]{:S(2)}) collective-permute-start(bf16[64,2048]{1,0:T(8,128)(2,1)} %get-tuple-element.197), channel_id=1, source_target_pairs={{64,0},{65,1},{66,2},{67,3},{68,4},{69,5},{70,6},{71,7},{72,8},{73... | collective-permute-start | bytes 786440 | tf_op jit(solution)/shard_map/ppermute | solution.py:47
  449.9 68.3 %reduce-scatter.6.cloned.1.call-start = ((), (), s32[]{:S(2)}) async-start(), calls=%async_computation.9 | async-start | bytes 5242880 | tf_op jit(solution)/shard_map/reduce_scatter | solution.py:367
  454.6 175.9 %reduce-scatter.4.cloned.1.call-start = ((), (), s32[]{:S(2)}) async-start(), calls=%async_computation.8 | async-start | bytes 15728640 | tf_op jit(solution)/shard_map/reduce_scatter | solution.py:364
  517.9 204.5 %reduce-scatter.8.cloned.1.call-start = ((), (), s32[]{:S(2)}) async-start(), calls=%async_computation.10 | async-start | bytes 4456448 | tf_op jit(solution)/shard_map/reduce_scatter | solution.py:75
  645.7 79.3 %copy-start.18 = (f32[2048]{0:T(1024)S(1)}, f32[2048]{0:T(1024)}, u32[]{:S(2)}) copy-start(f32[2048]{0:T(1024)} %copy-done.17) | copy-start | bytes 24580
  645.7 106.7 %all-gather.10.cloned.1.call-start = ((), (), s32[]{:S(2)}) async-start(), calls=%async_computation.12 | async-start | bytes 1310720 | tf_op jit(solution)/shard_map/all_gather | solution.py:85
  726.0 20.9 %all-to-all-start.3 = ((f32[64,1,2048]{2,1,0:T(1,128)}), f32[64,1,2048]{2,1,0:T(1,128)S(1)}, u32[]{:S(2)}, u32[]{:S(2)}) async-start(f32[64,1,2048]{2,1,0:T(1,128)} %broadcast_in_dim.29), calls=%async_computation.6 | async-start | bytes 1048576 | tf_op jit(solution)/shard_map/all_to_all | solution.py:35
  (11 other events, 93.5 us)
Sparse Core Ops, SparseCore 0:
  30.6 86.0 all-gather.7
  450.0 15.7 all-gather.5
  468.2 45.7 reduce-scatter.5
  518.0 112.5 reduce-scatter.3
  645.8 76.5 reduce-scatter.7
  725.1 27.2 all-gather.9
